TPU v7x, 256 devices: a whole 4x4x8 slice. The times are simulated.
256 devices in a mesh: tm: 32 (over z, y), row: 8 (over x, core).
Axes of the slice: x: 4, y: 4, z: 8, core: 2. Of those that a mesh axis runs over, the one named last changes fastest.
Arguments:
- tokens: bfloat16 [32768, 3072], P(('tm', 'row')), may hold values from -6 to 6
- w_qkv: bfloat16 [3072, 3, 3072], P(None, None, 'row'), may hold values from -1 to 1
- qk_gain: float32 [2, 3072], P(None, 'row'), may hold values from 0.5 to 6
- w_out: bfloat16 [3072, 3072], P('row'), may hold values from -0.109375 to 0.109375
- band_start: int32 [64, 5], replicated, may hold values from 0 to 2
Outputs:
- mixed: bfloat16 [32768, 3072], P(('tm', 'row'))
All inputs are finite; a program needn't handle non-finite values.
Results may differ from a plain program's by a relative error of at most 0.019.
Values may be sent and summed in bfloat16 or wider, within the bound.
A program may use at most 128 MiB of HBM per device.

v0:
```python
import math

import jax
import jax.numpy as jnp
from jax import lax
from jax.sharding import PartitionSpec as P

HD = 128
S = 512
SB = 128
WSLOT = 2
FR_DEV = 2


def with_halo(cells, sides, width):
    for axis, dim in sides:
        count = lax.axis_size(axis)
        ends = count - 1
        head = lax.slice_in_dim(cells, 0, width, axis=dim)
        tail = lax.slice_in_dim(cells, cells.shape[dim] - width, cells.shape[dim], axis=dim)
        cells = jnp.concatenate(
            [
                lax.ppermute(tail, axis, [(i, (i + 1) % count) for i in range(ends)]),
                cells,
                lax.ppermute(head, axis, [((i + 1) % count, i) for i in range(ends)]),
            ],
            axis=dim,
        )
    return cells


def shifted(value, axis, steps):
    count = lax.axis_size(axis)
    initial, last = (max(0, -steps), min(count, count - steps))
    return lax.ppermute(value, axis, [(source, source + steps) for source in range(initial, last)])


def normalize(columns, gain_row, head_count):
    shaped = columns.reshape(columns.shape[0], head_count, HD)
    factor = lax.rsqrt(jnp.mean(shaped * shaped, axis=-1, keepdims=True) + 1e-06)
    scaled = shaped * factor * gain_row.reshape(head_count, HD)
    return scaled.reshape(columns.shape[0], head_count * HD).astype(jnp.bfloat16)


def attend(query_rows, key_rows, value_rows, usable, head_count):
    query_heads = query_rows.reshape(query_rows.shape[0], head_count, HD)
    key_heads = key_rows.reshape(key_rows.shape[0], head_count, HD)
    value_heads = value_rows.reshape(value_rows.shape[0], head_count, HD)
    scores = jnp.einsum(
        "shd,khd->hsk", query_heads, key_heads, preferred_element_type=jnp.float32
    ) / math.sqrt(HD)
    scores = jnp.where(usable[None, None, :], scores, -1e30)
    row_max = jnp.max(scores, axis=-1, keepdims=True)
    weights = jnp.where(usable[None, None, :], jnp.exp(scores - row_max), 0.0)
    totals = jnp.sum(weights, axis=-1)
    probabilities = weights.astype(jnp.bfloat16)
    mixed = jnp.einsum(
        "hsk,khd->shd", probabilities, value_heads, preferred_element_type=jnp.float32
    )
    mixed = mixed / jnp.transpose(totals)[:, :, None]
    return mixed.reshape(query_rows.shape[0], head_count * HD).astype(jnp.bfloat16)


def shards(tokens, w_qkv, qk_gain, w_out, band_start):
    local_width = w_qkv.shape[2]
    local_heads = local_width // HD
    joined = w_qkv.reshape(w_qkv.shape[0], 3 * local_width)
    merged = jnp.dot(
        lax.all_gather(tokens, "row", axis=0, tiled=True),
        joined,
        preferred_element_type=jnp.float32,
    )
    projected = jnp.concatenate(
        [
            normalize(merged[:, :local_width], qk_gain[0], local_heads),
            normalize(merged[:, local_width : 2 * local_width], qk_gain[1], local_heads),
            merged[:, 2 * local_width :].astype(jnp.bfloat16),
        ],
        axis=1,
    )
    key_values = projected[:, local_width:].reshape(FR_DEV, S, 2 * local_width)
    nearby = with_halo(key_values, (("tm", 0),), 1)
    band_count = band_start.shape[1]
    frames_all = band_start.shape[0]
    my_index = lax.axis_index("tm")
    far_parts = [[None] * band_count for frame_slot in range(FR_DEV)]
    for level in range(band_count):
        rows_level = max(1, WSLOT // 2**level) * SB
        for direction in (1, -1):
            moved_by = direction * 2**level
            sender_frame = (level + 1) % 2 if direction > 0 else level % 2
            asking = jnp.clip((my_index + moved_by) * FR_DEV + sender_frame, 0, frames_all - 1)
            first_block = lax.dynamic_index_in_dim(band_start[:, level], asking, 0, keepdims=False)
            block = lax.dynamic_slice_in_dim(
                key_values[sender_frame], first_block * SB, rows_level, 0
            )
            far_parts[sender_frame][level] = shifted(block, "tm", moved_by)
    outputs = []
    for local_frame in range(FR_DEV):
        query_frame = my_index * FR_DEV + local_frame
        near_index = query_frame - 1 + jnp.arange(3, dtype=jnp.int32)
        near_valid = (near_index >= 0) & (near_index < frames_all)
        usable_parts = [jnp.repeat(near_valid, S)]
        for level in range(band_count):
            rows_level = max(1, WSLOT // 2**level) * SB
            sign = 1 if (local_frame + level) % 2 == 0 else -1
            key_frame = query_frame + sign * FR_DEV * 2**level
            inside = (key_frame >= 0) & (key_frame < frames_all)
            usable_parts.append(jnp.broadcast_to(inside, (rows_level,)))
        usable = jnp.concatenate(usable_parts)
        near_rows = nearby[local_frame : local_frame + 3].reshape(3 * S, 2 * local_width)
        all_rows = jnp.concatenate([near_rows] + far_parts[local_frame], axis=0)
        query_rows = projected[local_frame * S : (local_frame + 1) * S, :local_width]
        outputs.append(
            attend(
                query_rows,
                all_rows[:, :local_width],
                all_rows[:, local_width:],
                usable,
                local_heads,
            )
        )
    attended = jnp.concatenate(outputs, axis=0)
    return lax.psum_scatter(
        jnp.dot(attended, w_out, preferred_element_type=jnp.float32).astype(jnp.bfloat16),
        "row",
        scatter_dimension=0,
        tiled=True,
    )


def solution(mesh):
    placed = (P(("tm", "row"), None), P(None, None, "row"), P(None, "row"), P("row", None), P())
    return jax.shard_map(
        shards, mesh=mesh, in_specs=placed, out_specs=P(("tm", "row"), None), check_vma=False
    )
```

profile of v0, /device:TPU:1, one launch (start us, length us, event | category | flops | bytes accessed | tf_op | source)
XLA Modules:
  0.0 277.0 jit_solution(18206038895702916637)
XLA Ops:
  16.7 10.4 %copy.43 = bf16[3072,3,384]{0,2,1:T(8,128)(2,1)} copy(bf16[3072,3,384]{2,0,1:T(8,128)(2,1)} %param.6) | data formatting | bytes 14155776 | tf_op args[1]
  30.2 26.7 %all-gather.2.cloned.1.call-done = bf16[1024,3072]{1,0:T(8,128)(2,1)} async-done(((bf16[128,3072]{1,0:T(8,128)(2,1)}), bf16[1024,3072]{1,0:T(8,128)(2,1)}) %all-gather.2.cloned.1.call-update) | async-done | bytes 6291472 | tf_op jit(solution)/shard_map/all_gather | solution.py:69
  56.9 11.6 %fusion.52 = f32[1024,1152]{1,0:T(8,128)S(1)} fusion(bf16[1024,3072]{1,0:T(8,128)(2,1)} %all-gather.2.cloned.1.call-done, bf16[3072,1152]{0,1:T(8,128)(2,1)} %bitcast.59), kind=kOutput, calls=%fused_computation.93 | convolution fusion | flops 7247757312 | bytes 18087936 | tf_op jit(solution)/shard_map/dot_general | solution.py:68
  69.5 2.2 slice_multiply_fusion
  71.7 3.1 %copy.47 = f32[1024,384]{0,1:T(8,128)} copy(f32[1024,384]{1,0:T(8,128)} %get-tuple-element.9) | data formatting | bytes 3145728 | tf_op jit(solution)/shard_map/mul | solution.py:40
  77.8 3.1 %copy.48 = f32[1024,384]{1,0:T(8,128)} copy(f32[1024,384]{0,1:T(8,128)} %bitcast.62) | data formatting | bytes 3145728 | tf_op jit(solution)/shard_map/mul | solution.py:41
  80.9 3.1 %copy.44 = f32[1024,384]{0,1:T(8,128)} copy(f32[1024,384]{1,0:T(8,128)} %get-tuple-element.10) | data formatting | bytes 3145728 | tf_op jit(solution)/shard_map/mul | solution.py:40
  87.0 3.0 %copy.45 = f32[1024,384]{1,0:T(8,128)} copy(f32[1024,384]{0,1:T(8,128)} %bitcast.63) | data formatting | bytes 3145728 | tf_op jit(solution)/shard_map/mul | solution.py:41
  90.0 3.3 %multiply_convert_fusion = (bf16[1024,384]{1,0:T(8,128)(2,1)S(1)}, bf16[1024,384]{1,0:T(8,128)(2,1)S(1)}) fusion(f32[1024,384]{1,0:T(8,128)} %copy.48, f32[1024,1152]{1,0:T(8,128)} %copy-done.1, f32[384]{0:T(512)S(1)} %get-tuple-element.5, f32[384]{0:T(512)S(1)} %get-tuple-element.6, f32[1024,384]{1,0:T(8,128)} %copy.45), kind=kLoop, calls=%fused_computation.27 | loop fusion | flops 2359296 | bytes 7867392 | tf_op jit(solution)/shard_map/convert_element_type | solution.py:42
  94.5 4.0 %collective-permute-start = (bf16[1,512,768]{2,1,0:T(8,128)(2,1)}, bf16[1,512,768]{2,1,0:T(8,128)(2,1)}, u32[]{:S(2)}, u32[]{:S(2)}) collective-permute-start(bf16[1,512,768]{2,1,0:T(8,128)(2,1)} %bitcast.3), channel_id=1, source_target_pairs={{0,8},{8,16},{16,24},{24,32},{32,40},{40,48},{48,56},{56,64},{64,7... | collective-permute-start | bytes 2359304 | tf_op jit(solution)/shard_map/ppermute | solution.py:23
  99.8 1.8 constant_dynamic-slice_fusion.8
  101.6 4.7 %collective-permute-start.7 = (bf16[256,768]{1,0:T(8,128)(2,1)}, bf16[256,768]{1,0:T(8,128)(2,1)}, u32[]{:S(2)}, u32[]{:S(2)}) collective-permute-start(bf16[256,768]{1,0:T(8,128)(2,1)} %constant_dynamic-slice_fusion.8), channel_id=1, source_target_pairs={{0,8},{8,16},{16,24},{24,32},{32,40},{40,48},{48,56},{56,64},{64,7... | collective-permute-start | bytes 1179656 | tf_op jit(solution)/shard_map/ppermute | solution.py:35
  106.4 2.1 constant_dynamic-slice_fusion
  109.8 5.2 %collective-permute-start.9 = (bf16[128,768]{1,0:T(8,128)(2,1)}, bf16[128,768]{1,0:T(8,128)(2,1)}, u32[]{:S(2)}, u32[]{:S(2)}) collective-permute-start(bf16[128,768]{1,0:T(8,128)(2,1)} %get-tuple-element.27), channel_id=1, source_target_pairs={{0,32},{8,40},{16,48},{24,56},{32,64},{40,72},{48,80},{56,88},{64,... | collective-permute-start | bytes 589832 | tf_op jit(solution)/shard_map/ppermute | solution.py:35
  115.9 1.9 copy.54
  119.8 2.1 constant_dynamic-slice_fusion.10
  124.5 7.4 %collective-permute-start.11 = (bf16[128,768]{1,0:T(8,128)(2,1)S(1)}, bf16[128,768]{1,0:T(8,128)(2,1)S(1)}, u32[]{:S(2)}, u32[]{:S(2)}) collective-permute-start(bf16[128,768]{1,0:T(8,128)(2,1)S(1)} %copy-done.5), channel_id=1, source_target_pairs={{0,128},{8,136},{16,144},{24,152},{32,160},{40,168},{48,176},{56,1... | collective-permute-start | bytes 589832 | tf_op jit(solution)/shard_map/ppermute | solution.py:35
  136.0 8.1 %collective-permute-start.2 = (bf16[128,768]{1,0:T(8,128)(2,1)}, bf16[128,768]{1,0:T(8,128)(2,1)S(1)}, u32[]{:S(2)}, u32[]{:S(2)}) collective-permute-start(bf16[128,768]{1,0:T(8,128)(2,1)} %get-tuple-element.24), channel_id=1, source_target_pairs={{0,16},{8,24},{16,32},{24,40},{32,48},{40,56},{48,64},{56,72},{64,... | collective-permute-start | bytes 589832 | tf_op jit(solution)/shard_map/ppermute | solution.py:35
  147.4 8.2 %collective-permute-start.4 = (bf16[128,768]{1,0:T(8,128)(2,1)}, bf16[128,768]{1,0:T(8,128)(2,1)}, u32[]{:S(2)}, u32[]{:S(2)}) collective-permute-start(bf16[128,768]{1,0:T(8,128)(2,1)} %get-tuple-element.22), channel_id=1, source_target_pairs={{0,64},{8,72},{16,80},{24,88},{32,96},{40,104},{48,112},{56,120},{... | collective-permute-start | bytes 589832 | tf_op jit(solution)/shard_map/ppermute | solution.py:35
  156.9 2.1 fusion.47
  160.7 3.9 %copy.53 = bf16[2304,384]{0,1:T(8,128)(2,1)} copy(bf16[2304,384]{1,0:T(8,128)(2,1)} %get-tuple-element.14) | data formatting | bytes 3538944 | tf_op jit(solution)/shard_map/slice | solution.py:118
  164.5 3.9 %copy.55 = bf16[2304,384]{0,1:T(8,128)(2,1)} copy(bf16[2304,384]{1,0:T(8,128)(2,1)} %get-tuple-element.13) | data formatting | bytes 3538944 | tf_op jit(solution)/shard_map/slice | solution.py:117
  171.5 1.6 constant_dynamic-update-slice_fusion.1
  174.7 4.2 %fusion.46 = (bf16[2304,384]{1,0:T(8,128)(2,1)}, bf16[2304,384]{1,0:T(8,128)(2,1)}) fusion(bf16[2304,768]{1,0:T(8,128)(2,1)} %constant_dynamic-update-slice_fusion), kind=kLoop, calls=%fused_computation.87 | loop fusion | bytes 7077888 | tf_op jit(solution)/shard_map/slice | solution.py:117
  178.9 3.9 %copy.46 = bf16[2304,384]{0,1:T(8,128)(2,1)} copy(bf16[2304,384]{1,0:T(8,128)(2,1)} %get-tuple-element.12) | data formatting | bytes 3538944 | tf_op jit(solution)/shard_map/slice | solution.py:118
  182.8 3.8 %copy.50 = bf16[2304,384]{0,1:T(8,128)(2,1)} copy(bf16[2304,384]{1,0:T(8,128)(2,1)} %get-tuple-element.11) | data formatting | bytes 3538944 | tf_op jit(solution)/shard_map/slice | solution.py:117
  186.6 9.8 %fusion.50 = (f32[3,512]{1,0:T(4,128)S(1)}, bf16[3,512,2304]{2,1,0:T(8,128)(2,1)}) fusion(pred[2304]{0:T(1024)(128)(4,1)S(1)} %dynamic-update-slice.5, bf16[512,3,128]{0,2,1:T(8,128)(2,1)S(1)} %bitcast.70, bf16[2304,3,128]{0,2,1:T(8,128)(2,1)} %bitcast.66), kind=kOutput, calls=%fused_computation.91 | convolution fusion | flops 927205632 | bytes 9249024 | tf_op jit(solution)/shard_map/sub | solution.py:54
  196.4 6.0 %fusion.33 = bf16[512,3,128]{0,2,1:T(8,128)(2,1)S(1)} fusion(bf16[2304,3,128]{0,2,1:T(8,128)(2,1)} %bitcast.65, bf16[3,512,2304]{2,1,0:T(8,128)(2,1)} %get-tuple-element.45, f32[512,3]{0,1:T(4,128)S(1)} %bitcast.73), kind=kOutput, calls=%fused_computation.38 | convolution fusion | flops 906362880 | bytes 9246720 | tf_op jit(solution)/shard_map/hsk,khd->shd/dot_general | solution.py:57
  202.4 10.0 %fusion.51 = (f32[3,512]{1,0:T(4,128)S(1)}, bf16[3,512,2304]{2,1,0:T(8,128)(2,1)}) fusion(pred[2304]{0:T(1024)(128)(4,1)S(1)} %dynamic-update-slice.17, bf16[512,3,128]{0,2,1:T(8,128)(2,1)S(1)} %bitcast.69, bf16[2304,3,128]{0,2,1:T(8,128)(2,1)} %bitcast.68), kind=kOutput, calls=%fused_computation.92 | convolution fusion | flops 927205632 | bytes 9249024 | tf_op jit(solution)/shard_map/sub | solution.py:54
  212.4 5.9 %fusion.30 = bf16[512,3,128]{0,2,1:T(8,128)(2,1)S(1)} fusion(bf16[2304,3,128]{0,2,1:T(8,128)(2,1)} %bitcast.67, bf16[3,512,2304]{2,1,0:T(8,128)(2,1)} %get-tuple-element.47, f32[512,3]{0,1:T(4,128)S(1)} %bitcast.74), kind=kOutput, calls=%fused_computation.37 | convolution fusion | flops 906362880 | bytes 9246720 | tf_op jit(solution)/shard_map/hsk,khd->shd/dot_general | solution.py:57
  218.3 5.4 %convolution_convert_fusion = bf16[1024,3072]{1,0:T(8,128)(2,1)} fusion(bf16[384,3072]{1,0:T(8,128)(2,1)S(1)} %copy-done, bf16[512,384]{0,1:T(8,128)(2,1)S(1)} %bitcast.71, bf16[512,384]{0,1:T(8,128)(2,1)S(1)} %bitcast.72), kind=kOutput, calls=%fused_computation.18 | convolution fusion | flops 2420637696 | bytes 9437184 | tf_op jit(solution)/shard_map/dot_general | solution.py:125
  223.8 46.4 %reduce-scatter.2.cloned.1.call-done = bf16[128,3072]{1,0:T(8,128)(2,1)} async-done(((bf16[1024,3072]{1,0:T(8,128)(2,1)}), bf16[128,3072]{1,0:T(8,128)(2,1)}) %reduce-scatter.2.cloned.1.call-update) | async-done | bytes 786448 | tf_op jit(solution)/shard_map/reduce_scatter | solution.py:124
  (96 shorter events, 37.7 us)
Async XLA Ops:
  6.5 211.8 %copy-start = (bf16[384,3072]{1,0:T(8,128)(2,1)S(1)}, bf16[384,3072]{1,0:T(8,128)(2,1)}, u32[]{:S(2)}) copy-start(bf16[384,3072]{1,0:T(8,128)(2,1)} %param.8) | copy-start | bytes 7077892
  6.5 50.3 %all-gather.2.cloned.1.call-start = ((), (), s32[]{:S(2)}) async-start(), calls=%async_computation.1 | async-start | bytes 7077888 | tf_op jit(solution)/shard_map/all_gather | solution.py:69
  7.3 262.9 %reduce-scatter.2.cloned.1.call-start = ((), (), s32[]{:S(2)}) async-start(), calls=%async_computation.2 | async-start | bytes 7077888 | tf_op jit(solution)/shard_map/reduce_scatter | solution.py:124
  16.7 13.5 %copy-start.7 = (f32[2,384]{1,0:T(2,128)S(1)}, f32[2,384]{1,0:T(2,128)}, u32[]{:S(2)}) copy-start(f32[2,384]{1,0:T(2,128)} %param.7) | copy-start | bytes 9220
  68.4 3.3 %copy-start.1 = (f32[1024,1152]{1,0:T(8,128)}, f32[1024,1152]{1,0:T(8,128)S(1)}, u32[]{:S(2)}) copy-start(f32[1024,1152]{1,0:T(8,128)S(1)} %fusion.52) | copy-start | bytes 14155780
  90.0 3.3 %copy-start.2 = (bf16[1024,384]{1,0:T(8,128)(2,1)S(1)}, bf16[1024,384]{1,0:T(8,128)(2,1)}, u32[]{:S(2)}) copy-start(bf16[1024,384]{1,0:T(8,128)(2,1)} %slice.132) | copy-start | bytes 2359300
  94.5 28.6 %collective-permute-start = (bf16[1,512,768]{2,1,0:T(8,128)(2,1)}, bf16[1,512,768]{2,1,0:T(8,128)(2,1)}, u32[]{:S(2)}, u32[]{:S(2)}) collective-permute-start(bf16[1,512,768]{2,1,0:T(8,128)(2,1)} %bitcast.3), channel_id=1, source_target_pairs={{0,8},{8,16},{16,24},{24,32},{32,40},{40,48},{48,56},{56,64},{64,7... | collective-permute-start | bytes 2359304 | tf_op jit(solution)/shard_map/ppermute | solution.py:23
  98.6 26.0 %collective-permute-start.6 = (bf16[1,512,768]{2,1,0:T(8,128)(2,1)}, bf16[1,512,768]{2,1,0:T(8,128)(2,1)}, u32[]{:S(2)}, u32[]{:S(2)}) collective-permute-start(bf16[1,512,768]{2,1,0:T(8,128)(2,1)} %bitcast.19), channel_id=1, source_target_pairs={{8,0},{16,8},{24,16},{32,24},{40,32},{48,40},{56,48},{64,56},{72,6... | collective-permute-start | bytes 2359304 | tf_op jit(solution)/shard_map/ppermute | solution.py:25
  101.6 32.1 %collective-permute-start.7 = (bf16[256,768]{1,0:T(8,128)(2,1)}, bf16[256,768]{1,0:T(8,128)(2,1)}, u32[]{:S(2)}, u32[]{:S(2)}) collective-permute-start(bf16[256,768]{1,0:T(8,128)(2,1)} %constant_dynamic-slice_fusion.8), channel_id=1, source_target_pairs={{0,8},{8,16},{16,24},{24,32},{32,40},{40,48},{48,56},{56,64},{64,7... | collective-permute-start | bytes 1179656 | tf_op jit(solution)/shard_map/ppermute | solution.py:35
  108.5 27.5 %collective-permute-start.8 = (bf16[128,768]{1,0:T(8,128)(2,1)}, bf16[128,768]{1,0:T(8,128)(2,1)}, u32[]{:S(2)}, u32[]{:S(2)}) collective-permute-start(bf16[128,768]{1,0:T(8,128)(2,1)} %get-tuple-element.28), channel_id=1, source_target_pairs={{16,0},{24,8},{32,16},{40,24},{48,32},{56,40},{64,48},{72,56},{80,... | collective-permute-start | bytes 589832 | tf_op jit(solution)/shard_map/ppermute | solution.py:35
  109.8 35.3 %collective-permute-start.9 = (bf16[128,768]{1,0:T(8,128)(2,1)}, bf16[128,768]{1,0:T(8,128)(2,1)}, u32[]{:S(2)}, u32[]{:S(2)}) collective-permute-start(bf16[128,768]{1,0:T(8,128)(2,1)} %get-tuple-element.27), channel_id=1, source_target_pairs={{0,32},{8,40},{16,48},{24,56},{32,64},{40,72},{48,80},{56,88},{64,... | collective-permute-start | bytes 589832 | tf_op jit(solution)/shard_map/ppermute | solution.py:35
  118.7 4.5 %copy-start.6 = (bf16[128,768]{1,0:T(8,128)(2,1)S(1)}, bf16[128,768]{1,0:T(8,128)(2,1)}, u32[]{:S(2)}) copy-start(bf16[128,768]{1,0:T(8,128)(2,1)} %get-tuple-element.26) | copy-start | bytes 589828
  118.7 5.8 %copy-start.5 = (bf16[128,768]{1,0:T(8,128)(2,1)S(1)}, bf16[128,768]{1,0:T(8,128)(2,1)}, u32[]{:S(2)}) copy-start(bf16[128,768]{1,0:T(8,128)(2,1)} %get-tuple-element.25) | copy-start | bytes 589828
  123.2 24.1 %collective-permute-start.10 = (bf16[128,768]{1,0:T(8,128)(2,1)S(1)}, bf16[128,768]{1,0:T(8,128)(2,1)S(1)}, u32[]{:S(2)}, u32[]{:S(2)}) collective-permute-start(bf16[128,768]{1,0:T(8,128)(2,1)S(1)} %copy-done.6), channel_id=1, source_target_pairs={{64,0},{72,8},{80,16},{88,24},{96,32},{104,40},{112,48},{120,56},{... | collective-permute-start | bytes 589832 | tf_op jit(solution)/shard_map/ppermute | solution.py:35
  124.5 31.1 %collective-permute-start.11 = (bf16[128,768]{1,0:T(8,128)(2,1)S(1)}, bf16[128,768]{1,0:T(8,128)(2,1)S(1)}, u32[]{:S(2)}, u32[]{:S(2)}) collective-permute-start(bf16[128,768]{1,0:T(8,128)(2,1)S(1)} %copy-done.5), channel_id=1, source_target_pairs={{0,128},{8,136},{16,144},{24,152},{32,160},{40,168},{48,176},{56,1... | collective-permute-start | bytes 589832 | tf_op jit(solution)/shard_map/ppermute | solution.py:35
  133.7 34.7 %collective-permute-start.1 = (bf16[256,768]{1,0:T(8,128)(2,1)S(1)}, bf16[256,768]{1,0:T(8,128)(2,1)S(1)}, u32[]{:S(2)}, u32[]{:S(2)}) collective-permute-start(bf16[256,768]{1,0:T(8,128)(2,1)S(1)} %constant_dynamic-slice_fusion.18), channel_id=1, source_target_pairs={{8,0},{16,8},{24,16},{32,24},{40,32},{48,40},{56,48},{64,56},{72,6... | collective-permute-start | bytes 1179656 | tf_op jit(solution)/shard_map/ppermute | solution.py:35
  136.0 33.1 %collective-permute-start.2 = (bf16[128,768]{1,0:T(8,128)(2,1)}, bf16[128,768]{1,0:T(8,128)(2,1)S(1)}, u32[]{:S(2)}, u32[]{:S(2)}) collective-permute-start(bf16[128,768]{1,0:T(8,128)(2,1)} %get-tuple-element.24), channel_id=1, source_target_pairs={{0,16},{8,24},{16,32},{24,40},{32,48},{40,56},{48,64},{56,72},{64,... | collective-permute-start | bytes 589832 | tf_op jit(solution)/shard_map/ppermute | solution.py:35
  145.1 24.8 %collective-permute-start.3 = (bf16[128,768]{1,0:T(8,128)(2,1)}, bf16[128,768]{1,0:T(8,128)(2,1)}, u32[]{:S(2)}, u32[]{:S(2)}) collective-permute-start(bf16[128,768]{1,0:T(8,128)(2,1)} %get-tuple-element.23), channel_id=1, source_target_pairs={{32,0},{40,8},{48,16},{56,24},{64,32},{72,40},{80,48},{88,56},{96,... | collective-permute-start | bytes 589832 | tf_op jit(solution)/shard_map/ppermute | solution.py:35
  147.4 24.1 %collective-permute-start.4 = (bf16[128,768]{1,0:T(8,128)(2,1)}, bf16[128,768]{1,0:T(8,128)(2,1)}, u32[]{:S(2)}, u32[]{:S(2)}) collective-permute-start(bf16[128,768]{1,0:T(8,128)(2,1)} %get-tuple-element.22), channel_id=1, source_target_pairs={{0,64},{8,72},{16,80},{24,88},{32,96},{40,104},{48,112},{56,120},{... | collective-permute-start | bytes 589832 | tf_op jit(solution)/shard_map/ppermute | solution.py:35
  155.6 17.5 %collective-permute-start.5 = (bf16[128,768]{1,0:T(8,128)(2,1)}, bf16[128,768]{1,0:T(8,128)(2,1)}, u32[]{:S(2)}, u32[]{:S(2)}) collective-permute-start(bf16[128,768]{1,0:T(8,128)(2,1)} %get-tuple-element.21), channel_id=1, source_target_pairs={{128,0},{136,8},{144,16},{152,24},{160,32},{168,40},{176,48},{184,... | collective-permute-start | bytes 589832 | tf_op jit(solution)/shard_map/ppermute | solution.py:35
  178.9 7.7 %copy-start.4 = (bf16[512,384]{0,1:T(8,128)(2,1)S(1)}, bf16[512,384]{0,1:T(8,128)(2,1)}, u32[]{:S(2)}) copy-start(bf16[512,384]{0,1:T(8,128)(2,1)} %copy.54) | copy-start | bytes 1179652
  196.4 6.0 %copy-start.3 = (bf16[512,384]{0,1:T(8,128)(2,1)S(1)}, bf16[512,384]{0,1:T(8,128)(2,1)}, u32[]{:S(2)}) copy-start(bf16[512,384]{0,1:T(8,128)(2,1)} %copy.49) | copy-start | bytes 1179652
Sparse Core Ops, SparseCore 0:
  9.2 47.6 all-gather.1
  223.9 46.2 reduce-scatter.1
where the time goes:
time: 279 us; the launch traced here: 277 us
  local copies, waits for them, and re-layouts  76.1 us (27%)
  waiting for transfers between devices  73.8 us (26%)
  matrix products  48.7 us (17%)
  starting transfers between devices  45.5 us (16%)
  between operations  20.3 us (7%)
  other arithmetic  12.7 us (5%)
    reduce_scatter x1, waiting for transfers between devices, shards(): lax.psum_scatter(jnp.dot(attended, w_out, preferred_element_type=jnp.floa...  46.4 us
    ppermute x10, starting transfers between devices, shifted(): lax.ppermute(value, axis, [(source, source + steps) for source in range(i...  40.1 us
    all_gather x1, waiting for transfers between devices, shards(): lax.all_gather(tokens, 'row', axis=0, tiled=True)  26.7 us
    unnamed x37, local copies, waits for them, and re-layouts  22.1 us
    sub x2, matrix products, attend(): weights = jnp.where(usable[None, None, :], jnp.exp(scores - row_max), 0.0)  19.8 us
    slice x4, local copies, waits for them, and re-layouts, shards(): all_rows[:, :local_width]  14 us
    dot_general x2, matrix products, attend(): jnp.einsum('hsk,khd->shd', probabilities, value_heads, preferred_element_...  11.9 us
    dot_general x1, matrix products, shards(): jnp.dot(lax.all_gather(tokens, 'row', axis=0, tiled=True), joined, prefer...  11.6 us
  transfers between devices with their start and end apart: 14, of which 2 were waited for; matrix products, arithmetic and copies ran while one was open for 18% of the time, Pallas kernels for 0%

commit v1 on v0

v1 whole, which is shorter than its diff:
```python
import functools
import math

import jax
import jax.numpy as jnp
from jax import lax
from jax.experimental import pallas as pl
from jax.experimental.pallas import tpu as pltpu
from jax.sharding import PartitionSpec as P

MESH = pl.DeviceIdType.MESH
D = 3072
HD = 128
HL = 3
W = HL * HD
TB = 128
CH = 2 * TB
ROWS = 4 * CH
N_TM = 32
LO, OWN, HI, FAR, FAR4, BAND0 = 0, 512, 1536, 2048, 2816, 2944
KV_ROWS = 3456
QSCALE = math.log2(math.e) / math.sqrt(HD)
NEG = -1e30
KB = 256
F32 = jnp.float32
BF16 = jnp.bfloat16


def mo(value, by):
    return pl.multiple_of(value, by)


def kernel(
    tok, w3, gain, wout, band, out,
    G, WQ, WO, Q, KV, FS, ACC, MX, LS, S, PB, AF, A2, P0, P1, P2, P3, RU, RD, RL, RR,
    loc, sx, rx, sd, rd, sn, rn, sf, rf, sa, ra, sr, rr,
):
    tm = lax.axis_index("tm")
    row = lax.axis_index("row")
    x = row // 2
    c = row % 2
    right = (x + 1) % 4
    left = (x + 3) % 4
    across = (x + 2) % 4
    d_right = (tm, right * 2 + c)
    d_left = (tm, left * 2 + c)
    d_core = (tm, x * 2 + (1 - c))

    def d_tm(shift):
        return ((tm + shift + N_TM) % N_TM, row)

    loads = [pltpu.make_async_copy(tok, G.at[pl.ds(mo(row * TB, TB), TB)], loc.at[0])]
    for j in range(3):
        loads.append(pltpu.make_async_copy(w3.at[j], WQ.at[:, pl.ds(j * W, W)], loc.at[1 + j]))
    loads.append(pltpu.make_async_copy(wout, WO.at[pl.ds(0, W)], loc.at[4]))
    for load in loads:
        load.start()

    partners = [d_right, d_left, d_core, d_tm(1), d_tm(-1), d_tm(2), d_tm(-2),
                d_tm(4), d_tm(-4), d_tm(8), d_tm(-8), d_tm(16)]
    barrier = pltpu.get_barrier_semaphore()
    for device in partners:
        pl.semaphore_signal(barrier, inc=1, device_id=device, device_id_type=MESH)
    pl.semaphore_wait(barrier, len(partners))

    def remote(src, dst, send, recv, device):
        return pltpu.make_async_remote_copy(
            src_ref=src, dst_ref=dst, send_sem=send, recv_sem=recv,
            device_id=device, device_id_type=MESH)

    sent = []

    def send(src, dst, send_sem, recv_sem, device):
        copy = remote(src, dst, send_sem, recv_sem, device)
        copy.start()
        sent.append(copy)

    def arrived(dst, recv_sem, send_sem):
        remote(dst, dst, send_sem, recv_sem, d_core).wait_recv()

    H = TB // 2

    def half(xx, cc, part):
        return G.at[pl.ds(mo(((xx * 2 + cc) * 2 + part) * H, H), H)]

    send(tok.at[pl.ds(0, H)], half(x, c, 0), sx.at[0], rx.at[0], d_right)
    send(tok.at[pl.ds(H, H)], half(x, c, 1), sx.at[2], rx.at[2], d_left)
    send(tok, G.at[pl.ds(mo(row * TB, TB), TB)], sd.at[6], rd.at[6], d_core)
    send(tok.at[pl.ds(H, H)], half(x, c, 1), sx.at[1], rx.at[1], d_right)
    send(tok.at[pl.ds(0, H)], half(x, c, 0), sx.at[3], rx.at[3], d_left)
    send(wout, WO.at[pl.ds(W, W)], sd.at[7], rd.at[7], d_core)

    def pass_on(k, xx, part, device=None, k_next=None):
        piece = half(xx, c, part)
        arrived(piece, rx.at[k], sx.at[k])
        if device is not None:
            send(piece, piece, sx.at[k_next], rx.at[k_next], device)
        send(piece, piece, sd.at[k], rd.at[k], d_core)

    def from_core(k, xx, part):
        arrived(half(xx, 1 - c, part), rd.at[k], sd.at[k])

    gq = gain[0:1, :] * QSCALE
    gk = gain[1:2, :]

    def project(k, d):
        rows = pl.ds(mo(d * CH, CH), CH)
        kv_rows = pl.ds(mo(OWN + d * CH, CH), CH)
        merged = jnp.dot(G[rows, :], WQ[...], preferred_element_type=F32)
        for g, gains in enumerate((gq, gk)):
            for h in range(HL):
                v = merged[:, g * W + h * HD: g * W + (h + 1) * HD]
                factor = lax.rsqrt(jnp.mean(v * v, axis=1, keepdims=True) + 1e-6)
                v = (v * factor * gains[:, h * HD:(h + 1) * HD]).astype(BF16)
                if g == 0:
                    Q[rows, h * HD:(h + 1) * HD] = v
                else:
                    KV[kv_rows, h * HD:(h + 1) * HD] = v
        KV[kv_rows, W:] = merged[:, 2 * W:].astype(BF16)
        frame = d // 2
        there = KV.at[pl.ds(mo((1 - frame) * HI + (d - 2 * frame) * CH, CH), CH)]
        send(KV.at[kv_rows], there, sn.at[k], rn.at[k], d_tm(2 * frame - 1))

    def far_slot(frame, level):
        if level == 4:
            return KV.at[pl.ds(FAR4, TB)]
        return KV.at[pl.ds(mo(FAR + frame * 3 * TB + (level - 1) * TB, TB), TB)]

    def chosen(base, n, first):
        at = [KV[pl.ds(mo(base + i * TB, TB), n), :] for i in range(3)]
        return jnp.where(first == 0, at[0], jnp.where(first == 1, at[1], at[2]))

    def send_far(frame, level, k, moved_by):
        asking = ((tm + moved_by + N_TM) % N_TM) * 2 + frame
        FS[k] = chosen(OWN + frame * 512, TB, band[asking, level])
        copy = remote(FS.at[k], far_slot(frame, level), sf.at[k], rf.at[k], d_tm(moved_by))
        copy.start()
        return copy

    def send_far_frame(frame, half_at):
        for level in (3, 2, 1):
            sign = 2 * ((level + frame) % 2) - 1
            sent.append(send_far(frame, level, 3 * half_at + level - 1, sign * 2 ** level))

    frame4 = 1 - tm // 16
    mine = x // 2

    loads[0].wait()
    for load in loads[1:4]:
        load.wait()
    arrived(G.at[pl.ds(mo((x * 2 + 1 - c) * TB, TB), TB)], rd.at[6], sd.at[6])
    project(0, x)

    pass_on(0, left, 0, d_right, 4)
    pass_on(2, right, 1, d_left, 5)
    pass_on(1, left, 1)
    pass_on(3, right, 0)
    for k, xx, part in ((0, left, 0), (1, left, 1), (2, right, 1), (3, right, 0)):
        from_core(k, xx, part)
    near_first = x + 1 - 2 * (x % 2)
    project(1, near_first)
    @pl.when(frame4 == mine)
    def _():
        send_far(mine, 4, 6, 16)

    send_far_frame(mine, 0)
    project(2, (near_first + 2) % 4)
    pass_on(4, across, 0)
    pass_on(5, across, 1)
    from_core(4, across, 0)
    from_core(5, across, 1)
    project(3, across)

    @pl.when(frame4 != mine)
    def _():
        send_far(1 - mine, 4, 6, 16)

    send_far_frame(1 - mine, 1)

    for k in range(4):
        d = (x, near_first, (near_first + 2) % 4, across)[k]
        frame = d // 2
        arrived(KV.at[pl.ds(mo((1 - frame) * HI + (d - 2 * frame) * CH, CH), CH)], rn.at[k], sn.at[k])

    def score_tiles(rows, lanes, tiles):
        q = Q[rows, lanes]
        top = None
        for t, (first, valid) in enumerate(tiles):
            keys = KV[pl.ds(first, KB), lanes]
            s = lax.dot_general(q, keys, (((1,), (1,)), ((), ())), preferred_element_type=F32)
            if valid is not None:
                s = jnp.where(valid, s, NEG)
            S[:, t * KB:(t + 1) * KB] = s
            both = jnp.maximum(s[:, :HD], s[:, HD:])
            top = both if top is None else jnp.maximum(top, both)
        return top

    def weigh_tiles(tiles, lanes_v, m):
        total = None
        acc = None
        for t, (first, _) in enumerate(tiles):
            p = jnp.exp2(S[:, t * KB:(t + 1) * KB] - m)
            both = p[:, :HD] + p[:, HD:]
            total = both if total is None else total + both
            part = jnp.dot(p.astype(BF16), KV[pl.ds(first, KB), lanes_v], preferred_element_type=F32)
            acc = part if acc is None else acc + part
        return total, acc

    for frame in range(2):
        KV[BAND0 + frame * KB:BAND0 + (frame + 1) * KB, :] = chosen((1 - frame) * HI, KB, band[tm * 2 + frame, 0])

    below = tm > 0
    above = tm < N_TM - 1

    @pl.loop(0, 4)
    def _(d):
        frame = d // 2
        rows = pl.ds(mo(d * CH, CH), CH)
        near_ok = jnp.logical_or(jnp.logical_and(frame == 0, below), jnp.logical_and(frame == 1, above))
        band_ok = jnp.logical_or(jnp.logical_and(frame == 1, below), jnp.logical_and(frame == 0, above))
        tiles = [(OWN + i * KB, None) for i in range(4)]
        tiles += [(mo(frame * HI + i * KB, KB), near_ok) for i in range(2)]
        tiles += [(mo(BAND0 + frame * KB, TB), band_ok)]
        for h in range(HL):
            lanes = slice(h * HD, (h + 1) * HD)
            top = score_tiles(rows, lanes, tiles)
            m = jnp.broadcast_to(jnp.max(top, axis=1, keepdims=True), (CH, HD))
            total, acc = weigh_tiles(tiles, slice(W + h * HD, W + (h + 1) * HD), m[:, :1])
            MX[rows, lanes] = m
            LS[rows, lanes] = total
            ACC[rows, lanes] = acc

    for half_at in range(2):
        frame = mine if half_at == 0 else 1 - mine
        for level in (3, 2, 1):
            k = 3 * half_at + level - 1
            arrived(far_slot(frame, level), rf.at[k], sf.at[k])
    arrived(far_slot(0, 4), rf.at[6], sf.at[6])
    loads[4].wait()
    arrived(WO.at[pl.ds(W, W)], rd.at[7], sd.at[7])

    def far_ok(frame, level):
        other = tm + (1 - 2 * ((frame + level) % 2)) * 2 ** level
        return jnp.logical_and(other >= 0, other < N_TM)

    def finish(step, d):
        frame = d // 2
        rows = pl.ds(mo(d * CH, CH), CH)
        segs = [(mo(FAR + frame * 3 * TB + (level - 1) * TB, TB), far_ok(frame, level)) for level in (1, 2, 3)]
        segs.append((FAR4, far_ok(frame, 4)))
        for h in range(HL):
            lanes = slice(h * HD, (h + 1) * HD)
            lanes_v = slice(W + h * HD, W + (h + 1) * HD)
            q = Q[rows, lanes]
            m_old = MX[rows, lanes]
            scores = []
            top = None
            for first, valid in segs:
                s = lax.dot_general(q, KV[pl.ds(first, TB), lanes], (((1,), (1,)), ((), ())),
                                    preferred_element_type=F32)
                s = jnp.where(valid, s, NEG)
                scores.append(s)
                top = s if top is None else jnp.maximum(top, s)
            m = jnp.maximum(m_old, jnp.max(top, axis=1, keepdims=True))
            scale = jnp.exp2(m_old - m)
            total = LS[rows, lanes] * scale
            acc = ACC[rows, lanes] * scale
            for s, (first, _) in zip(scores, segs):
                p = jnp.exp2(s - m)
                total = total + p
                acc = acc + jnp.dot(p.astype(BF16), KV[pl.ds(first, TB), lanes_v], preferred_element_type=F32)
            AF[step, :, lanes] = (acc / jnp.sum(total, axis=1, keepdims=True)).astype(BF16)
        send(AF.at[step, pl.ds(mo((1 - c) * TB, TB), TB)], A2.at[step, :, pl.ds(W, W)],
             sa.at[step], ra.at[step], d_core)
        A2[step, :, :W] = AF[step, pl.ds(mo(c * TB, TB), TB), :]
        arrived(A2.at[step, :, pl.ds(W, W)], ra.at[step], sa.at[step])

    NB = 512

    def product(step, lo, n, cols):
        return jnp.dot(A2[step, lo:lo + n, :], WO[:, cols], preferred_element_type=F32)

    columns = [slice(i * NB, (i + 1) * NB) for i in range(D // NB)]

    finish(0, across)
    for cols in columns:
        P0[:, cols] = product(0, 0, TB, cols).astype(BF16)
    send(P0.at[pl.ds(0, H)], RU, sr.at[0], rr.at[0], d_right)
    send(P0.at[pl.ds(H, H)], RD, sr.at[1], rr.at[1], d_left)

    finish(1, right)
    for cols in columns:
        P1[:, cols] = product(1, 0, TB, cols).astype(BF16)
    send(P1.at[pl.ds(H, H)], RL.at[pl.ds(H, H)], sr.at[2], rr.at[2], d_right)
    finish(2, left)
    for cols in columns:
        P2[:, cols] = product(2, 0, TB, cols).astype(BF16)
    send(P2.at[pl.ds(0, H)], RR.at[pl.ds(0, H)], sr.at[3], rr.at[3], d_left)

    arrived(RU, rr.at[0], sr.at[0])
    P1[0:H, :] = (P1[0:H, :].astype(F32) + RU[...].astype(F32)).astype(BF16)
    send(P1.at[pl.ds(0, H)], RL.at[pl.ds(0, H)], sr.at[4], rr.at[4], d_right)
    arrived(RD, rr.at[1], sr.at[1])
    P2[H:, :] = (P2[H:, :].astype(F32) + RD[...].astype(F32)).astype(BF16)
    send(P2.at[pl.ds(H, H)], RR.at[pl.ds(H, H)], sr.at[5], rr.at[5], d_left)

    finish(3, x)
    for cols in columns:
        P3[:, cols] = product(3, 0, TB, cols)
    arrived(RL.at[pl.ds(H, H)], rr.at[2], sr.at[2])
    arrived(RR.at[pl.ds(0, H)], rr.at[3], sr.at[3])
    arrived(RL.at[pl.ds(0, H)], rr.at[4], sr.at[4])
    arrived(RR.at[pl.ds(H, H)], rr.at[5], sr.at[5])
    out[...] = (P3[...] + RL[...].astype(F32) + RR[...].astype(F32)).astype(BF16)

    for copy in sent:
        copy.wait_send()
    remote(FS.at[6], far_slot(0, 4), sf.at[6], rf.at[6], d_tm(16)).wait_send()


def shards(tokens, w_qkv, qk_gain, w_out, band_start):
    w3 = jnp.transpose(w_qkv, (1, 0, 2))
    vmem = pl.BlockSpec(memory_space=pltpu.VMEM)
    hbm = pl.BlockSpec(memory_space=pl.ANY)
    dma = pltpu.SemaphoreType.DMA
    return pl.pallas_call(
        kernel,
        out_shape=jax.ShapeDtypeStruct((TB, D), BF16),
        in_specs=[hbm, hbm, vmem, hbm, pl.BlockSpec(memory_space=pltpu.SMEM)],
        out_specs=vmem,
        scratch_shapes=[
            pltpu.VMEM((ROWS, D), BF16),
            pltpu.VMEM((D, 3 * W), BF16),
            pltpu.VMEM((2 * W, D), BF16),
            pltpu.VMEM((ROWS, W), BF16),
            pltpu.VMEM((KV_ROWS, 2 * W), BF16),
            pltpu.VMEM((7, TB, 2 * W), BF16),
            pltpu.VMEM((ROWS, W), F32),
            pltpu.VMEM((ROWS, W), F32),
            pltpu.VMEM((ROWS, W), F32),
            pltpu.VMEM((CH, 7 * KB), F32),
            pltpu.VMEM((16, 128), BF16),
            pltpu.VMEM((4, CH, W), BF16),
            pltpu.VMEM((4, TB, 2 * W), BF16),
            pltpu.VMEM((TB, D), BF16),
            pltpu.VMEM((TB, D), BF16),
            pltpu.VMEM((TB, D), BF16),
            pltpu.VMEM((TB, D), F32),
            pltpu.VMEM((TB // 2, D), BF16),
            pltpu.VMEM((TB // 2, D), BF16),
            pltpu.VMEM((TB, D), BF16),
            pltpu.VMEM((TB, D), BF16),
            dma((5,)), dma((6,)), dma((6,)), dma((8,)), dma((8,)), dma((4,)), dma((4,)),
            dma((7,)), dma((7,)), dma((4,)), dma((4,)), dma((6,)), dma((6,)),
        ],
        compiler_params=pltpu.CompilerParams(
            collective_id=0, has_side_effects=True, vmem_limit_bytes=60 * 2**20),
        cost_estimate=pl.CostEstimate(flops=14 * 10**9, bytes_accessed=12 * 10**6, transcendentals=7 * 10**6),
        name="band_attention",
    )(tokens, w3, qk_gain, w_out, band_start)


def solution(mesh):
    placed = (P(("tm", "row"), None), P(None, None, "row"), P(None, "row"), P("row", None), P())
    return jax.shard_map(
        shards, mesh=mesh, in_specs=placed, out_specs=P(("tm", "row"), None), check_vma=False
    )
```

time: 279 us -> 123 us (0.44)
  Pallas kernels: 0 us -> 118 us
  waiting for transfers between devices: 73.8 us -> 0 us
  local copies, waits for them, and re-layouts: 76.1 us -> 3.45 us
  matrix products: 48.7 us -> 0 us
  starting transfers between devices: 45.5 us -> 0 us
  between operations: 20.3 us -> 0.01 us
  other arithmetic: 12.7 us -> 0 us
    pallas_call x0 -> x1, Pallas kernels: none -> 118 us  [shards(): pl.pallas_call(kernel, out_shape=jax.ShapeDtypeStruct((TB, D), BF16), in_...]
    reduce_scatter x1 -> x0, waiting for transfers between devices: 46.4 us -> none  [shards(): lax.psum_scatter(jnp.dot(attended, w_out, preferred_element_type=jnp.floa...]
    ppermute x12 -> x0, starting transfers between devices: 45.4 us -> none  [the longest x10 40.1 us: shifted(): lax.ppermute(value, axis, [(source, source + steps) for source in range(i...]
    dot_general x4 -> x0, matrix products: 28.9 us -> none  [the longest x2 11.9 us: attend(): jnp.einsum('hsk,khd->shd', probabilities, value_heads, preferred_element_...]
    slice x12 -> x0, local copies, waits for them, and re-layouts: 27.4 us -> none  [the longest x4 14 us: shards(): all_rows[:, :local_width]]
    all_gather x1 -> x0, waiting for transfers between devices: 26.7 us -> none  [shards(): lax.all_gather(tokens, 'row', axis=0, tiled=True)]
    sub x2 -> x0, matrix products: 19.8 us -> none  [attend(): weights = jnp.where(usable[None, None, :], jnp.exp(scores - row_max), 0.0)]
    unnamed x37 -> x2, local copies, waits for them, and re-layouts: 22.1 us -> 3.45 us
  transfers between devices with their start and end apart: 14 -> 0, of which waited for: 2 -> 0; matrix products, arithmetic and copies ran while one was open for 18% -> 0% of each run, Pallas kernels for 0% -> 0%
where the time goes in v1:
time: 123 us; the launch traced here: 122 us
  Pallas kernels  118 us (96%)
  local copies, waits for them, and re-layouts  3.45 us (3%)
    pallas_call x1, Pallas kernels, shards(): pl.pallas_call(kernel, out_shape=jax.ShapeDtypeStruct((TB, D), BF16), in_...  118 us
    unnamed x2, local copies, waits for them, and re-layouts  3.45 us

profile of v1, /device:TPU:1, one launch (start us, length us, event | category | flops | bytes accessed | tf_op | source)
XLA Modules:
  0.0 121.9 jit_solution(3989137821080337000)
XLA Ops:
  0.0 1.4 %copy.6.band = s32[64,5]{1,0:T(8,128)} copy(s32[64,5]{0,1:T(8,128)} %param.9) | data formatting | bytes 2560 | tf_op args[4]
  1.4 118.4 %band_attention.1 = bf16[128,3072]{1,0:T(8,128)(2,1)} custom-call(bf16[128,3072]{1,0:T(8,128)(2,1)} %tok.1, bf16[3,3072,384]{2,1,0:T(8,128)(2,1)} %bitcast.1, f32[2,384]{1,0:T(2,128)} %gain.1, bf16[384,3072]{1,0:T(8,128)(2,1)} %wout.1, s32[64,5]{1,0:T(8,128)} %copy.6.band), custom_call_target="tpu_custom_call" | custom-call | flops 14000000000 | bytes 12000000 | tf_op jit(solution)/shard_map/band_attention/pallas_call | solution.py:326
  119.8 2.1 %copy.8 = bf16[128,3072]{1,0:T(8,128)(2,1)} copy(bf16[128,3072]{1,0:T(8,128)(2,1)} %band_attention.1) | data formatting | bytes 1572864

commit v2 on v1

v2 whole, which is shorter than its diff:
```python
import functools
import math

import jax
import jax.numpy as jnp
from jax import lax
from jax.experimental import pallas as pl
from jax.experimental.pallas import tpu as pltpu
from jax.sharding import PartitionSpec as P

MESH = pl.DeviceIdType.MESH
D = 3072
HD = 128
HL = 3
W = HL * HD
TB = 128
CH = 2 * TB
ROWS = 4 * CH
N_TM = 32
LO, OWN, HI, FAR, FAR4, BAND0 = 0, 512, 1536, 2048, 2816, 2944
KV_ROWS = 3456
QSCALE = math.log2(math.e) / math.sqrt(HD)
NEG = -1e30
KB = 256
F32 = jnp.float32
BF16 = jnp.bfloat16


def mo(value, by):
    return pl.multiple_of(value, by)


def kernel(
    tok, w3, gain, wout, band, out,
    G, GH, WQ, WO, Q, KV, FS, ACC, MX, LS, S, AF, A2, P0, P1, P2, P3, RU, RD, RL, RR,
    loc, sx, rx, sd, rd, sn, rn, sf, rf, sa, ra, sr, rr,
):
    tm = lax.axis_index("tm")
    row = lax.axis_index("row")
    x = row // 2
    c = row % 2
    right = (x + 1) % 4
    left = (x + 3) % 4
    across = (x + 2) % 4
    d_right = (tm, right * 2 + c)
    d_left = (tm, left * 2 + c)
    d_core = (tm, x * 2 + (1 - c))

    def d_tm(shift):
        return ((tm + shift + N_TM) % N_TM, row)

    loads = [pltpu.make_async_copy(tok, G.at[pl.ds(mo(row * TB, TB), TB)], loc.at[0])]
    for j in range(3):
        loads.append(pltpu.make_async_copy(w3.at[j], WQ.at[:, pl.ds(j * W, W)], loc.at[1 + j]))
    loads.append(pltpu.make_async_copy(wout, WO.at[pl.ds(0, W)], loc.at[4]))
    for load in loads:
        load.start()

    partners = [d_right, d_left, d_core, d_tm(1), d_tm(-1), d_tm(2), d_tm(-2),
                d_tm(4), d_tm(-4), d_tm(8), d_tm(-8), d_tm(16)]
    barrier = pltpu.get_barrier_semaphore()
    for device in partners:
        pl.semaphore_signal(barrier, inc=1, device_id=device, device_id_type=MESH)
    loads[0].wait()
    pl.semaphore_wait(barrier, len(partners))

    def remote(src, dst, send, recv, device):
        return pltpu.make_async_remote_copy(
            src_ref=src, dst_ref=dst, send_sem=send, recv_sem=recv,
            device_id=device, device_id_type=MESH)

    sent = []

    def send(src, dst, send_sem, recv_sem, device):
        copy = remote(src, dst, send_sem, recv_sem, device)
        copy.start()
        sent.append(copy)

    def arrived(dst, recv_sem, send_sem):
        remote(dst, dst, send_sem, recv_sem, d_core).wait_recv()

    H = TB // 2

    def gather(G, base):
        def block(xx, cc):
            return G.at[pl.ds(mo((xx * 2 + cc) * TB, TB), TB)]

        def half(xx, part, cc=c):
            return G.at[pl.ds(mo(((xx * 2 + cc) * 2 + part) * H, H), H)]

        def pass_on(k, xx, part, device=None, k_next=None):
            piece = half(xx, part)
            arrived(piece, rx.at[base + k], sx.at[base + k])
            if device is not None:
                send(piece, piece, sx.at[base + k_next], rx.at[base + k_next], device)
            send(piece, piece, sd.at[base + k], rd.at[base + k], d_core)

        def from_core(k, xx, part):
            arrived(half(xx, part, 1 - c), rd.at[base + k], sd.at[base + k])

        def begin():
            send(half(x, 0), half(x, 0), sx.at[base], rx.at[base], d_right)
            send(half(x, 1), half(x, 1), sx.at[base + 2], rx.at[base + 2], d_left)
            send(block(x, c), block(x, c), sd.at[base + 6], rd.at[base + 6], d_core)
            send(half(x, 1), half(x, 1), sx.at[base + 1], rx.at[base + 1], d_right)
            send(half(x, 0), half(x, 0), sx.at[base + 3], rx.at[base + 3], d_left)

        def first():
            arrived(block(x, 1 - c), rd.at[base + 6], sd.at[base + 6])

        def middle():
            pass_on(0, left, 0, d_right, 4)
            pass_on(2, right, 1, d_left, 5)
            pass_on(1, left, 1)
            pass_on(3, right, 0)
            for k, xx, part in ((0, left, 0), (1, left, 1), (2, right, 1), (3, right, 0)):
                from_core(k, xx, part)

        def last():
            pass_on(4, across, 0)
            pass_on(5, across, 1)
            from_core(4, across, 0)
            from_core(5, across, 1)

        return begin, first, middle, last

    own = G.at[pl.ds(mo(row * TB, TB), TB)]
    begin, first, middle, last = gather(G, 0)
    begin_halo, first_halo, middle_halo, last_halo = gather(GH, 7)
    begin()
    own_halo = GH.at[pl.ds(mo(row * TB, TB), TB)]
    send(own, own_halo, sn.at[0], rn.at[0], d_tm(2 * (x // 2) - 1))

    gq = gain[0:1, :] * QSCALE
    gk = gain[1:2, :]

    def normed(v, gains):
        factor = lax.rsqrt(jnp.mean(v * v, axis=1, keepdims=True) + 1e-6)
        return (v * factor * gains).astype(BF16)

    def project(tokens, first_row, d):
        merged = jnp.dot(tokens[pl.ds(mo(d * CH, CH), CH), :], WQ[:, W:], preferred_element_type=F32)
        rows = pl.ds(mo(first_row, CH), CH)
        for h in range(HL):
            lanes = slice(h * HD, (h + 1) * HD)
            KV[rows, lanes] = normed(merged[:, lanes], gk[:, lanes])
        KV[rows, W:] = merged[:, W:].astype(BF16)

    def project_own(d):
        project(G, OWN + d * CH, d)

    def project_halo(d):
        frame = d // 2
        project(GH, (1 - frame) * HI + (d - 2 * frame) * CH, d)

    def far_slot(frame, level):
        if level == 4:
            return KV.at[pl.ds(FAR4, TB)]
        return KV.at[pl.ds(mo(FAR + frame * 3 * TB + (level - 1) * TB, TB), TB)]

    def chosen(base, n, first):
        at = [KV[pl.ds(mo(base + i * TB, TB), n), :] for i in range(3)]
        return jnp.where(first == 0, at[0], jnp.where(first == 1, at[1], at[2]))

    def send_far(frame, level, k, moved_by):
        asking = ((tm + moved_by + N_TM) % N_TM) * 2 + frame
        FS[k] = chosen(OWN + frame * 512, TB, band[level, asking])
        copy = remote(FS.at[k], far_slot(frame, level), sf.at[k], rf.at[k], d_tm(moved_by))
        copy.start()
        return copy

    def send_far_frame(frame, half_at):
        for level in (1, 2, 3):
            sign = 2 * ((level + frame) % 2) - 1
            sent.append(send_far(frame, level, 3 * half_at + level - 1, sign * 2 ** level))

    frame4 = 1 - tm // 16
    mine = x // 2

    for load in loads[2:4]:
        load.wait()
    first()
    project_own(x)
    middle()
    near_first = x + 1 - 2 * (x % 2)
    near_other = (near_first + 2) % 4
    project_own(near_first)

    @pl.when(frame4 == mine)
    def _():
        send_far(mine, 4, 6, 16)

    send_far_frame(mine, 0)
    project_own(near_other)
    arrived(own_halo, rn.at[0], sn.at[0])
    begin_halo()
    last()
    project_own(across)

    @pl.when(frame4 != mine)
    def _():
        send_far(1 - mine, 4, 6, 16)

    send_far_frame(1 - mine, 1)
    loads[4].wait()
    send(WO.at[pl.ds(0, W)], WO.at[pl.ds(W, W)], sd.at[14], rd.at[14], d_core)

    loads[1].wait()

    @pl.loop(0, 2)
    def _(i):
        rows = pl.ds(mo(i * 512, 512), 512)
        merged = jnp.dot(G[rows, :], WQ[:, :W], preferred_element_type=F32)
        for h in range(HL):
            lanes = slice(h * HD, (h + 1) * HD)
            Q[rows, lanes] = normed(merged[:, lanes], gq[:, lanes])

    def score_tiles(rows, lanes, tiles, top=None):
        q = Q[rows, lanes]
        at = 0
        for begins, n, valid in tiles:
            s = lax.dot_general(q, KV[pl.ds(begins, n), lanes], (((1,), (1,)), ((), ())), preferred_element_type=F32)
            if valid is not None:
                s = jnp.where(valid, s, NEG)
            S[:, at:at + n] = s
            at += n
            for i in range(0, n, HD):
                top = s[:, i:i + HD] if top is None else jnp.maximum(top, s[:, i:i + HD])
        return top

    def weigh_tiles(tiles, lanes_v, m, total=None, acc=None):
        at = 0
        for begins, n, _ in tiles:
            p = jnp.exp2(S[:, at:at + n] - m)
            at += n
            for i in range(0, n, HD):
                total = p[:, i:i + HD] if total is None else total + p[:, i:i + HD]
            part = jnp.dot(p.astype(BF16), KV[pl.ds(begins, n), lanes_v], preferred_element_type=F32)
            acc = part if acc is None else acc + part
        return total, acc

    @pl.loop(0, 4)
    def _(d):
        rows = pl.ds(mo(d * CH, CH), CH)
        tiles = [(OWN + i * KB, KB, None) for i in range(4)]
        for h in range(HL):
            lanes = slice(h * HD, (h + 1) * HD)
            top = score_tiles(rows, lanes, tiles)
            m = jnp.broadcast_to(jnp.max(top, axis=1, keepdims=True), (CH, HD))
            total, acc = weigh_tiles(tiles, slice(W + h * HD, W + (h + 1) * HD), m[:, :1])
            MX[rows, lanes] = m
            LS[rows, lanes] = total
            ACC[rows, lanes] = acc

    first_halo()
    project_halo(x)
    middle_halo()
    project_halo(near_first)
    project_halo(near_other)
    last_halo()
    project_halo(across)
    for frame in range(2):
        KV[BAND0 + frame * KB:BAND0 + (frame + 1) * KB, :] = chosen((1 - frame) * HI, KB, band[0, tm * 2 + frame])

    for half_at in range(2):
        frame = mine if half_at == 0 else 1 - mine
        for level in (3, 2, 1):
            k = 3 * half_at + level - 1
            arrived(far_slot(frame, level), rf.at[k], sf.at[k])
    arrived(far_slot(0, 4), rf.at[6], sf.at[6])
    arrived(WO.at[pl.ds(W, W)], rd.at[14], sd.at[14])

    def far_ok(frame, level):
        other = tm + (1 - 2 * ((frame + level) % 2)) * 2 ** level
        return jnp.logical_and(other >= 0, other < N_TM)

    def near_ok(frame):
        other = tm + 2 * frame - 1
        return jnp.logical_and(other >= 0, other < N_TM)

    def finish(step, d):
        frame = d // 2
        rows = pl.ds(mo(d * CH, CH), CH)
        tiles = [(mo(frame * HI + i * KB, KB), KB, near_ok(frame)) for i in range(2)]
        tiles += [(mo(BAND0 + frame * KB, TB), KB, near_ok(1 - frame))]
        tiles += [(mo(FAR + frame * 3 * TB + (level - 1) * TB, TB), TB, far_ok(frame, level)) for level in (1, 2, 3)]
        tiles += [(FAR4, TB, far_ok(frame, 4))]
        for h in range(HL):
            lanes = slice(h * HD, (h + 1) * HD)
            lanes_v = slice(W + h * HD, W + (h + 1) * HD)
            top = score_tiles(rows, lanes, tiles)
            m_old = MX[rows, lanes]
            m = jnp.maximum(m_old, jnp.max(top, axis=1, keepdims=True))
            scale = jnp.exp2(m_old - m)
            total, acc = weigh_tiles(tiles, lanes_v, m[:, :1], LS[rows, lanes] * scale, ACC[rows, lanes] * scale)
            AF[step, :, lanes] = (acc / jnp.sum(total, axis=1, keepdims=True)).astype(BF16)
        send(AF.at[step, pl.ds(mo((1 - c) * TB, TB), TB)], A2.at[step, :, pl.ds(W, W)],
             sa.at[step], ra.at[step], d_core)
        A2[step, :, :W] = AF[step, pl.ds(mo(c * TB, TB), TB), :]
        arrived(A2.at[step, :, pl.ds(W, W)], ra.at[step], sa.at[step])

    NB = 512

    def product(step, lo, n, cols):
        return jnp.dot(A2[step, lo:lo + n, :], WO[:, cols], preferred_element_type=F32)

    columns = [slice(i * NB, (i + 1) * NB) for i in range(D // NB)]

    finish(0, across)
    for cols in columns:
        P0[:, cols] = product(0, 0, TB, cols).astype(BF16)
    send(P0.at[pl.ds(0, H)], RU, sr.at[0], rr.at[0], d_right)
    send(P0.at[pl.ds(H, H)], RD, sr.at[1], rr.at[1], d_left)

    finish(1, right)
    for cols in columns:
        P1[:, cols] = product(1, 0, TB, cols).astype(BF16)
    send(P1.at[pl.ds(H, H)], RL.at[pl.ds(H, H)], sr.at[2], rr.at[2], d_right)
    finish(2, left)
    for cols in columns:
        P2[:, cols] = product(2, 0, TB, cols).astype(BF16)
    send(P2.at[pl.ds(0, H)], RR.at[pl.ds(0, H)], sr.at[3], rr.at[3], d_left)

    arrived(RU, rr.at[0], sr.at[0])
    P1[0:H, :] = (P1[0:H, :].astype(F32) + RU[...].astype(F32)).astype(BF16)
    send(P1.at[pl.ds(0, H)], RL.at[pl.ds(0, H)], sr.at[4], rr.at[4], d_right)
    arrived(RD, rr.at[1], sr.at[1])
    P2[H:, :] = (P2[H:, :].astype(F32) + RD[...].astype(F32)).astype(BF16)
    send(P2.at[pl.ds(H, H)], RR.at[pl.ds(H, H)], sr.at[5], rr.at[5], d_left)

    finish(3, x)
    for cols in columns:
        P3[:, cols] = product(3, 0, TB, cols)
    arrived(RL.at[pl.ds(H, H)], rr.at[2], sr.at[2])
    arrived(RR.at[pl.ds(0, H)], rr.at[3], sr.at[3])
    arrived(RL.at[pl.ds(0, H)], rr.at[4], sr.at[4])
    arrived(RR.at[pl.ds(H, H)], rr.at[5], sr.at[5])
    out[...] = (P3[...] + RL[...].astype(F32) + RR[...].astype(F32)).astype(BF16)

    for copy in sent:
        copy.wait_send()
    remote(FS.at[6], far_slot(0, 4), sf.at[6], rf.at[6], d_tm(16)).wait_send()


def shards(tokens, w_qkv, qk_gain, w_out, band_start):
    w3 = jnp.transpose(w_qkv, (1, 0, 2))
    vmem = pl.BlockSpec(memory_space=pltpu.VMEM)
    hbm = pl.BlockSpec(memory_space=pl.ANY)
    dma = pltpu.SemaphoreType.DMA
    return pl.pallas_call(
        kernel,
        out_shape=jax.ShapeDtypeStruct((TB, D), BF16),
        in_specs=[hbm, hbm, vmem, hbm, pl.BlockSpec(memory_space=pltpu.SMEM)],
        out_specs=vmem,
        scratch_shapes=[
            pltpu.VMEM((ROWS, D), BF16),
            pltpu.VMEM((ROWS, D), BF16),
            pltpu.VMEM((D, 3 * W), BF16),
            pltpu.VMEM((2 * W, D), BF16),
            pltpu.VMEM((ROWS, W), BF16),
            pltpu.VMEM((KV_ROWS, 2 * W), BF16),
            pltpu.VMEM((7, TB, 2 * W), BF16),
            pltpu.VMEM((ROWS, W), F32),
            pltpu.VMEM((ROWS, W), F32),
            pltpu.VMEM((ROWS, W), F32),
            pltpu.VMEM((CH, 5 * KB), F32),
            pltpu.VMEM((4, CH, W), BF16),
            pltpu.VMEM((4, TB, 2 * W), BF16),
            pltpu.VMEM((TB, D), BF16),
            pltpu.VMEM((TB, D), BF16),
            pltpu.VMEM((TB, D), BF16),
            pltpu.VMEM((TB, D), F32),
            pltpu.VMEM((TB // 2, D), BF16),
            pltpu.VMEM((TB // 2, D), BF16),
            pltpu.VMEM((TB, D), BF16),
            pltpu.VMEM((TB, D), BF16),
            dma((5,)), dma((13,)), dma((13,)), dma((15,)), dma((15,)), dma((1,)), dma((1,)),
            dma((7,)), dma((7,)), dma((4,)), dma((4,)), dma((6,)), dma((6,)),
        ],
        compiler_params=pltpu.CompilerParams(
            collective_id=0, has_side_effects=True, vmem_limit_bytes=60 * 2**20),
        cost_estimate=pl.CostEstimate(flops=14 * 10**9, bytes_accessed=12 * 10**6, transcendentals=7 * 10**6),
        name="band_attention",
    )(tokens, w3, qk_gain, w_out, jnp.transpose(band_start))


def solution(mesh):
    placed = (P(("tm", "row"), None), P(None, None, "row"), P(None, "row"), P("row", None), P())
    return jax.shard_map(
        shards, mesh=mesh, in_specs=placed, out_specs=P(("tm", "row"), None), check_vma=False
    )
```

time: 123 us -> 105 us (0.85); the launches traced: 122 us -> 105 us
  Pallas kernels: 118 us -> 103 us
  local copies, waits for them, and re-layouts: 3.45 us -> 2.06 us
    pallas_call x1, Pallas kernels: 118 us -> 103 us  [shards(): pl.pallas_call(kernel, out_shape=jax.ShapeDtypeStruct((TB, D), BF16), in_...]
    unnamed x2 -> x1, local copies, waits for them, and re-layouts: 3.45 us -> 2.06 us
where the time goes in v2:
time: 105 us
  Pallas kernels  103 us (98%)
  local copies, waits for them, and re-layouts  2.06 us (2%)
    pallas_call x1, Pallas kernels, shards(): pl.pallas_call(kernel, out_shape=jax.ShapeDtypeStruct((TB, D), BF16), in_...  103 us

profile of v2, /device:TPU:1, one launch (start us, length us, event | category | flops | bytes accessed | tf_op | source)
XLA Modules:
  0.0 105.2 jit_solution(183802419341769820)
XLA Ops:
  0.0 103.1 %band_attention.1 = bf16[128,3072]{1,0:T(8,128)(2,1)} custom-call(bf16[128,3072]{1,0:T(8,128)(2,1)} %tok.1, bf16[3,3072,384]{2,1,0:T(8,128)(2,1)} %bitcast.2, f32[2,384]{1,0:T(2,128)} %gain.1, bf16[384,3072]{1,0:T(8,128)(2,1)} %wout.1, s32[5,64]{1,0:T(8,128)} %bitcast.3), custom_call_target="tpu_custom_call" | custom-call | flops 14000000000 | bytes 12000000 | tf_op jit(solution)/shard_map/band_attention/pallas_call | solution.py:350
  103.1 2.1 %copy.7 = bf16[128,3072]{1,0:T(8,128)(2,1)} copy(bf16[128,3072]{1,0:T(8,128)(2,1)} %band_attention.1) | data formatting | bytes 1572864

commit v3 on v2

--- a/solution.py
+++ b/solution.py
@@ -21,6 +21,7 @@
 KV_ROWS = 3456
 QSCALE = math.log2(math.e) / math.sqrt(HD)
 NEG = -1e30
+NR = 96
 KB = 256
 F32 = jnp.float32
 BF16 = jnp.bfloat16
@@ -33,7 +34,7 @@
 def kernel(
     tok, w3, gain, wout, band, out,
     G, GH, WQ, WO, Q, KV, FS, ACC, MX, LS, S, AF, A2, P0, P1, P2, P3, RU, RD, RL, RR,
-    loc, sx, rx, sd, rd, sn, rn, sf, rf, sa, ra, sr, rr,
+    loc, sx, rx, sd, rd, sn, rn, sf, rf, sa, ra, sr, rr, known,
 ):
     tm = lax.axis_index("tm")
     row = lax.axis_index("row")
@@ -56,13 +57,43 @@
     for load in loads:
         load.start()
 
-    partners = [d_right, d_left, d_core, d_tm(1), d_tm(-1), d_tm(2), d_tm(-2),
-                d_tm(4), d_tm(-4), d_tm(8), d_tm(-8), d_tm(16)]
+    def signal(semaphore, device):
+        pl.semaphore_signal(semaphore, inc=1, device_id=device, device_id_type=MESH)
+
+    KV[FAR:, W:] = jnp.zeros((KV_ROWS - FAR, W), BF16)
+    for block in range(4):
+        for first in (LO, HI):
+            KV[first + block * TB + NR:first + (block + 1) * TB, W:] = jnp.zeros((TB - NR, W), BF16)
+
+    def inside(shift):
+        return jnp.logical_and(tm + shift >= 0, tm + shift < N_TM)
+
+    def count(*shifts):
+        total = 0
+        for shift in shifts:
+            total = total + inside(shift).astype(jnp.int32)
+        return total
+
     barrier = pltpu.get_barrier_semaphore()
-    for device in partners:
-        pl.semaphore_signal(barrier, inc=1, device_id=device, device_id_type=MESH)
+    for device in (d_right, d_left, d_core):
+        signal(barrier, device)
+
+    def signal_tm(semaphore, shift):
+        @pl.when(inside(shift))
+        def _():
+            signal(semaphore, d_tm(shift))
+
+    signal_tm(barrier, 1)
+    signal_tm(barrier, -1)
     loads[0].wait()
-    pl.semaphore_wait(barrier, len(partners))
+    pl.semaphore_wait(barrier, 3 + count(1, -1))
+
+    def tell(level):
+        signal_tm(known.at[level], 2 ** level)
+        signal_tm(known.at[level], -(2 ** level))
+
+    def heard(level):
+        pl.semaphore_wait(known.at[level], count(2 ** level, -(2 ** level)))
 
     def remote(src, dst, send, recv, device):
         return pltpu.make_async_remote_copy(
@@ -76,14 +107,32 @@
         copy.start()
         sent.append(copy)
 
+    sent_if = []
+
+    def send_if(here, src, dst, send_sem, recv_sem, device):
+        copy = remote(src, dst, send_sem, recv_sem, device)
+
+        @pl.when(here)
+        def _():
+            copy.start()
+
+        sent_if.append((here, copy))
+
+    def arrived_if(here, dst, recv_sem, send_sem):
+        @pl.when(here)
+        def _():
+            arrived(dst, recv_sem, send_sem)
+
     def arrived(dst, recv_sem, send_sem):
         remote(dst, dst, send_sem, recv_sem, d_core).wait_recv()
 
     H = TB // 2
 
-    def gather(G, base):
+    def gather(G, n, base):
+        H = n // 2
+
         def block(xx, cc):
-            return G.at[pl.ds(mo((xx * 2 + cc) * TB, TB), TB)]
+            return G.at[pl.ds(mo((xx * 2 + cc) * n, n), n)]
 
         def half(xx, part, cc=c):
             return G.at[pl.ds(mo(((xx * 2 + cc) * 2 + part) * H, H), H)]
@@ -125,11 +174,21 @@
         return begin, first, middle, last
 
     own = G.at[pl.ds(mo(row * TB, TB), TB)]
-    begin, first, middle, last = gather(G, 0)
-    begin_halo, first_halo, middle_halo, last_halo = gather(GH, 7)
+    begin, first, middle, last = gather(G, TB, 0)
+    begin_halo, first_halo, middle_halo, last_halo = gather(GH, NR, 7)
     begin()
-    own_halo = GH.at[pl.ds(mo(row * TB, TB), TB)]
-    send(own, own_halo, sn.at[0], rn.at[0], d_tm(2 * (x // 2) - 1))
+    tell(0)
+    own_halo = GH.at[pl.ds(mo(row * NR, NR), NR)]
+    own_part = G.at[pl.ds(mo(row * TB, TB), NR)]
+    up = 2 * (x // 2) - 1
+    send_if(inside(up), own_part, own_halo, sn.at[0], rn.at[0], d_tm(up))
+
+    @pl.when(jnp.logical_not(inside(-up)))
+    def _():
+        filler = pltpu.make_async_copy(own_part, own_halo, loc.at[0])
+        filler.start()
+        filler.wait()
+
 
     gq = gain[0:1, :] * QSCALE
     gk = gain[1:2, :]
@@ -138,20 +197,32 @@
         factor = lax.rsqrt(jnp.mean(v * v, axis=1, keepdims=True) + 1e-6)
         return (v * factor * gains).astype(BF16)
 
-    def project(tokens, first_row, d):
-        merged = jnp.dot(tokens[pl.ds(mo(d * CH, CH), CH), :], WQ[:, W:], preferred_element_type=F32)
-        rows = pl.ds(mo(first_row, CH), CH)
-        for h in range(HL):
-            lanes = slice(h * HD, (h + 1) * HD)
-            KV[rows, lanes] = normed(merged[:, lanes], gk[:, lanes])
-        KV[rows, W:] = merged[:, W:].astype(BF16)
-
-    def project_own(d):
-        project(G, OWN + d * CH, d)
+    def project(tokens, n, first_row):
+        merged = jnp.dot(tokens, WQ[:, W:], preferred_element_type=F32)
+        for cc in range(2):
+            rows = pl.ds(mo(first_row + cc * TB, TB), n)
+            mine = merged[cc * n:(cc + 1) * n]
+            for h in range(HL):
+                lanes = slice(h * HD, (h + 1) * HD)
+                KV[rows, lanes] = normed(mine[:, lanes], gk[:, lanes])
+            KV[rows, W:] = mine[:, W:].astype(BF16)
+
+    def halo_row(d):
+        frame = d // 2
+        return (1 - frame) * HI + (d - 2 * frame) * CH
+
+    def near_piece(d, cc):
+        return KV.at[pl.ds(mo(halo_row(d) + cc * TB + NR, 16), TB - NR)]
+
+    def project_own(k, d):
+        project(G[pl.ds(mo(d * CH, CH), CH), :], TB, OWN + d * CH)
+        for cc in range(2):
+            to = 2 * (d // 2) - 1
+            send_if(inside(to), KV.at[pl.ds(mo(OWN + d * CH + cc * TB + NR, 16), TB - NR)], near_piece(d, cc),
+                    sn.at[1 + 2 * k + cc], rn.at[1 + 2 * k + cc], d_tm(to))
 
     def project_halo(d):
-        frame = d // 2
-        project(GH, (1 - frame) * HI + (d - 2 * frame) * CH, d)
+        project(GH[pl.ds(mo(d * 2 * NR, 2 * NR), 2 * NR), :], NR, halo_row(d))
 
     def far_slot(frame, level):
         if level == 4:
@@ -162,17 +233,16 @@
         at = [KV[pl.ds(mo(base + i * TB, TB), n), :] for i in range(3)]
         return jnp.where(first == 0, at[0], jnp.where(first == 1, at[1], at[2]))
 
-    def send_far(frame, level, k, moved_by):
+    def stage_far(frame, level, k, moved_by):
         asking = ((tm + moved_by + N_TM) % N_TM) * 2 + frame
         FS[k] = chosen(OWN + frame * 512, TB, band[level, asking])
-        copy = remote(FS.at[k], far_slot(frame, level), sf.at[k], rf.at[k], d_tm(moved_by))
-        copy.start()
-        return copy
-
-    def send_far_frame(frame, half_at):
-        for level in (1, 2, 3):
-            sign = 2 * ((level + frame) % 2) - 1
-            sent.append(send_far(frame, level, 3 * half_at + level - 1, sign * 2 ** level))
+
+    def send_far(half_at, level):
+        frame = mine if half_at == 0 else 1 - mine
+        moved_by = (2 * ((level + frame) % 2) - 1) * 2 ** level
+        k = 3 * half_at + level - 1
+        stage_far(frame, level, k, moved_by)
+        send_if(inside(moved_by), FS.at[k], far_slot(frame, level), sf.at[k], rf.at[k], d_tm(moved_by))
 
     frame4 = 1 - tm // 16
     mine = x // 2
@@ -180,28 +250,31 @@
     for load in loads[2:4]:
         load.wait()
     first()
-    project_own(x)
+    project_own(0, x)
+    heard(0)
+    tell(1)
     middle()
+    heard(1)
+    tell(2)
     near_first = x + 1 - 2 * (x % 2)
     near_other = (near_first + 2) % 4
-    project_own(near_first)
-
-    @pl.when(frame4 == mine)
-    def _():
-        send_far(mine, 4, 6, 16)
-
-    send_far_frame(mine, 0)
-    project_own(near_other)
-    arrived(own_halo, rn.at[0], sn.at[0])
+    project_own(1, near_first)
+    send_far(0, 2)
+    send_far(0, 1)
+    project_own(2, near_other)
+    arrived_if(inside(-up), own_halo, rn.at[0], sn.at[0])
     begin_halo()
+    heard(2)
+    tell(3)
+    send_far(0, 3)
     last()
-    project_own(across)
-
-    @pl.when(frame4 != mine)
-    def _():
-        send_far(1 - mine, 4, 6, 16)
-
-    send_far_frame(1 - mine, 1)
+    project_own(3, across)
+    send_far(1, 3)
+    heard(3)
+    stage_far(frame4, 4, 6, 16)
+    send(FS.at[6], far_slot(0, 4), sf.at[6], rf.at[6], d_tm(16))
+    send_far(1, 2)
+    send_far(1, 1)
     loads[4].wait()
     send(WO.at[pl.ds(0, W)], WO.at[pl.ds(W, W)], sd.at[14], rd.at[14], d_core)
 
@@ -259,24 +332,25 @@
     project_halo(near_other)
     last_halo()
     project_halo(across)
+    for k, d in enumerate((x, near_first, near_other, across)):
+        for cc in range(2):
+            arrived_if(inside(1 - 2 * (d // 2)), near_piece(d, cc), rn.at[1 + 2 * k + cc], sn.at[1 + 2 * k + cc])
     for frame in range(2):
         KV[BAND0 + frame * KB:BAND0 + (frame + 1) * KB, :] = chosen((1 - frame) * HI, KB, band[0, tm * 2 + frame])
+
+    def far_ok(frame, level):
+        return inside((1 - 2 * ((frame + level) % 2)) * 2 ** level)
+
+    def near_ok(frame):
+        return inside(2 * frame - 1)
 
     for half_at in range(2):
         frame = mine if half_at == 0 else 1 - mine
         for level in (3, 2, 1):
             k = 3 * half_at + level - 1
-            arrived(far_slot(frame, level), rf.at[k], sf.at[k])
+            arrived_if(far_ok(frame, level), far_slot(frame, level), rf.at[k], sf.at[k])
     arrived(far_slot(0, 4), rf.at[6], sf.at[6])
     arrived(WO.at[pl.ds(W, W)], rd.at[14], sd.at[14])
-
-    def far_ok(frame, level):
-        other = tm + (1 - 2 * ((frame + level) % 2)) * 2 ** level
-        return jnp.logical_and(other >= 0, other < N_TM)
-
-    def near_ok(frame):
-        other = tm + 2 * frame - 1
-        return jnp.logical_and(other >= 0, other < N_TM)
 
     def finish(step, d):
         frame = d // 2
@@ -339,7 +413,10 @@
 
     for copy in sent:
         copy.wait_send()
-    remote(FS.at[6], far_slot(0, 4), sf.at[6], rf.at[6], d_tm(16)).wait_send()
+    for here, copy in sent_if:
+        @pl.when(here)
+        def _(copy=copy):
+            copy.wait_send()
 
 
 def shards(tokens, w_qkv, qk_gain, w_out, band_start):
@@ -354,7 +431,7 @@
         out_specs=vmem,
         scratch_shapes=[
             pltpu.VMEM((ROWS, D), BF16),
-            pltpu.VMEM((ROWS, D), BF16),
+            pltpu.VMEM((8 * NR, D), BF16),
             pltpu.VMEM((D, 3 * W), BF16),
             pltpu.VMEM((2 * W, D), BF16),
             pltpu.VMEM((ROWS, W), BF16),
@@ -374,8 +451,9 @@
             pltpu.VMEM((TB // 2, D), BF16),
             pltpu.VMEM((TB, D), BF16),
             pltpu.VMEM((TB, D), BF16),
-            dma((5,)), dma((13,)), dma((13,)), dma((15,)), dma((15,)), dma((1,)), dma((1,)),
+            dma((5,)), dma((13,)), dma((13,)), dma((15,)), dma((15,)), dma((9,)), dma((9,)),
             dma((7,)), dma((7,)), dma((4,)), dma((4,)), dma((6,)), dma((6,)),
+            pltpu.SemaphoreType.REGULAR((4,)),
         ],
         compiler_params=pltpu.CompilerParams(
             collective_id=0, has_side_effects=True, vmem_limit_bytes=60 * 2**20),

time: 105 us -> 97 us (0.924)
  Pallas kernels: 103 us -> 94.8 us
    pallas_call x1, Pallas kernels: 103 us -> 94.8 us  [shards(): pl.pallas_call(kernel, out_shape=jax.ShapeDtypeStruct((TB, D), BF16), in_...]
where the time goes in v3:
time: 97 us; the launch traced here: 96.9 us
  Pallas kernels  94.8 us (98%)
  local copies, waits for them, and re-layouts  2.06 us (2%)
    pallas_call x1, Pallas kernels, shards(): pl.pallas_call(kernel, out_shape=jax.ShapeDtypeStruct((TB, D), BF16), in_...  94.8 us
    unnamed x1, local copies, waits for them, and re-layouts  2.06 us

profile of v3, /device:TPU:1, one launch (start us, length us, event | category | flops | bytes accessed | tf_op | source)
XLA Modules:
  0.0 96.9 jit_solution(1528941605745037862)
XLA Ops:
  0.0 94.8 %band_attention.1 = bf16[128,3072]{1,0:T(8,128)(2,1)} custom-call(bf16[128,3072]{1,0:T(8,128)(2,1)} %tok.1, bf16[3,3072,384]{2,1,0:T(8,128)(2,1)} %bitcast.2, f32[2,384]{1,0:T(2,128)} %gain.1, bf16[384,3072]{1,0:T(8,128)(2,1)} %wout.1, s32[5,64]{1,0:T(8,128)} %bitcast.3), custom_call_target="tpu_custom_call" | custom-call | flops 14000000000 | bytes 12000000 | tf_op jit(solution)/shard_map/band_attention/pallas_call | solution.py:427
  94.8 2.1 %copy.7 = bf16[128,3072]{1,0:T(8,128)(2,1)} copy(bf16[128,3072]{1,0:T(8,128)(2,1)} %band_attention.1) | data formatting | bytes 1572864

commit v4 on v3

--- a/solution.py
+++ b/solution.py
@@ -21,7 +21,7 @@
 KV_ROWS = 3456
 QSCALE = math.log2(math.e) / math.sqrt(HD)
 NEG = -1e30
-NR = 96
+NR = 112
 KB = 256
 F32 = jnp.float32
 BF16 = jnp.bfloat16
@@ -33,7 +33,7 @@
 
 def kernel(
     tok, w3, gain, wout, band, out,
-    G, GH, WQ, WO, Q, KV, FS, ACC, MX, LS, S, AF, A2, P0, P1, P2, P3, RU, RD, RL, RR,
+    G, GH, WQ, WO, Q, KV, FS, ACC, MX, LS, OUT, S, AF, A2, P0, P1, P2, P3, RU, RD, RL, RR,
     loc, sx, rx, sd, rd, sn, rn, sf, rf, sa, ra, sr, rr, known,
 ):
     tm = lax.axis_index("tm")
@@ -129,13 +129,13 @@
     H = TB // 2
 
     def gather(G, n, base):
-        H = n // 2
+        cut = (n // 2 + 15) // 16 * 16
 
         def block(xx, cc):
             return G.at[pl.ds(mo((xx * 2 + cc) * n, n), n)]
 
         def half(xx, part, cc=c):
-            return G.at[pl.ds(mo(((xx * 2 + cc) * 2 + part) * H, H), H)]
+            return G.at[pl.ds(mo((xx * 2 + cc) * n + part * cut, 16), (cut, n - cut)[part])]
 
         def pass_on(k, xx, part, device=None, k_next=None):
             piece = half(xx, part)
@@ -162,6 +162,8 @@
             pass_on(2, right, 1, d_left, 5)
             pass_on(1, left, 1)
             pass_on(3, right, 0)
+
+        def middle_core():
             for k, xx, part in ((0, left, 0), (1, left, 1), (2, right, 1), (3, right, 0)):
                 from_core(k, xx, part)
 
@@ -171,11 +173,11 @@
             from_core(4, across, 0)
             from_core(5, across, 1)
 
-        return begin, first, middle, last
+        return begin, first, middle, middle_core, last
 
     own = G.at[pl.ds(mo(row * TB, TB), TB)]
-    begin, first, middle, last = gather(G, TB, 0)
-    begin_halo, first_halo, middle_halo, last_halo = gather(GH, NR, 7)
+    begin, first, middle, middle_core, last = gather(G, TB, 0)
+    begin_halo, first_halo, middle_halo, middle_core_halo, last_halo = gather(GH, NR, 7)
     begin()
     tell(0)
     own_halo = GH.at[pl.ds(mo(row * NR, NR), NR)]
@@ -256,6 +258,7 @@
     middle()
     heard(1)
     tell(2)
+    middle_core()
     near_first = x + 1 - 2 * (x % 2)
     near_other = (near_first + 2) % 4
     project_own(1, near_first)
@@ -312,8 +315,7 @@
             acc = part if acc is None else acc + part
         return total, acc
 
-    @pl.loop(0, 4)
-    def _(d):
+    def attend_own(d):
         rows = pl.ds(mo(d * CH, CH), CH)
         tiles = [(OWN + i * KB, KB, None) for i in range(4)]
         for h in range(HL):
@@ -325,9 +327,13 @@
             LS[rows, lanes] = total
             ACC[rows, lanes] = acc
 
+    pl.loop(0, 2)(attend_own)
+    middle_halo()
+    pl.loop(2, 4)(attend_own)
+
     first_halo()
     project_halo(x)
-    middle_halo()
+    middle_core_halo()
     project_halo(near_first)
     project_halo(near_other)
     last_halo()
@@ -344,55 +350,77 @@
     def near_ok(frame):
         return inside(2 * frame - 1)
 
-    for half_at in range(2):
-        frame = mine if half_at == 0 else 1 - mine
-        for level in (3, 2, 1):
-            k = 3 * half_at + level - 1
-            arrived_if(far_ok(frame, level), far_slot(frame, level), rf.at[k], sf.at[k])
-    arrived(far_slot(0, 4), rf.at[6], sf.at[6])
+    def far_arrived():
+        for half_at in range(2):
+            frame = mine if half_at == 0 else 1 - mine
+            for level in (3, 2, 1):
+                k = 3 * half_at + level - 1
+                arrived_if(far_ok(frame, level), far_slot(frame, level), rf.at[k], sf.at[k])
+        arrived(far_slot(0, 4), rf.at[6], sf.at[6])
+
     arrived(WO.at[pl.ds(W, W)], rd.at[14], sd.at[14])
 
     def finish(step, d):
         frame = d // 2
         rows = pl.ds(mo(d * CH, CH), CH)
-        tiles = [(mo(frame * HI + i * KB, KB), KB, near_ok(frame)) for i in range(2)]
-        tiles += [(mo(BAND0 + frame * KB, TB), KB, near_ok(1 - frame))]
-        tiles += [(mo(FAR + frame * 3 * TB + (level - 1) * TB, TB), TB, far_ok(frame, level)) for level in (1, 2, 3)]
-        tiles += [(FAR4, TB, far_ok(frame, 4))]
-        for h in range(HL):
+        near = [(mo(frame * HI + i * KB, KB), KB, near_ok(frame)) for i in range(2)]
+        near += [(mo(BAND0 + frame * KB, TB), KB, near_ok(1 - frame))]
+        far = [(mo(FAR + frame * 3 * TB + (level - 1) * TB, TB), TB, far_ok(frame, level)) for level in (1, 2, 3)]
+        far += [(FAR4, TB, far_ok(frame, 4))]
+
+        def merge(h, tiles):
             lanes = slice(h * HD, (h + 1) * HD)
-            lanes_v = slice(W + h * HD, W + (h + 1) * HD)
             top = score_tiles(rows, lanes, tiles)
             m_old = MX[rows, lanes]
             m = jnp.maximum(m_old, jnp.max(top, axis=1, keepdims=True))
             scale = jnp.exp2(m_old - m)
-            total, acc = weigh_tiles(tiles, lanes_v, m[:, :1], LS[rows, lanes] * scale, ACC[rows, lanes] * scale)
+            total, acc = weigh_tiles(tiles, slice(W + h * HD, W + (h + 1) * HD), m[:, :1],
+                                     LS[rows, lanes] * scale, ACC[rows, lanes] * scale)
+            return lanes, m, total, acc
+
+        if step == 0:
+            for h in range(HL):
+                lanes, m, total, acc = merge(h, near)
+                MX[rows, lanes] = m
+                LS[rows, lanes] = total
+                ACC[rows, lanes] = acc
+            far_arrived()
+            near = []
+        for h in range(HL):
+            lanes, _, total, acc = merge(h, near + far)
             AF[step, :, lanes] = (acc / jnp.sum(total, axis=1, keepdims=True)).astype(BF16)
         send(AF.at[step, pl.ds(mo((1 - c) * TB, TB), TB)], A2.at[step, :, pl.ds(W, W)],
              sa.at[step], ra.at[step], d_core)
         A2[step, :, :W] = AF[step, pl.ds(mo(c * TB, TB), TB), :]
+
+    def exchanged(step):
         arrived(A2.at[step, :, pl.ds(W, W)], ra.at[step], sa.at[step])
 
     NB = 512
 
-    def product(step, lo, n, cols):
-        return jnp.dot(A2[step, lo:lo + n, :], WO[:, cols], preferred_element_type=F32)
+    def product(step, cols, heads=slice(0, 2 * W)):
+        return jnp.dot(A2[step, :, heads], WO[heads, cols], preferred_element_type=F32)
 
     columns = [slice(i * NB, (i + 1) * NB) for i in range(D // NB)]
 
     finish(0, across)
     for cols in columns:
-        P0[:, cols] = product(0, 0, TB, cols).astype(BF16)
+        P3[:, cols] = product(0, cols, slice(0, W))
+    exchanged(0)
+    for cols in columns:
+        P0[:, cols] = (P3[:, cols] + product(0, cols, slice(W, 2 * W))).astype(BF16)
     send(P0.at[pl.ds(0, H)], RU, sr.at[0], rr.at[0], d_right)
     send(P0.at[pl.ds(H, H)], RD, sr.at[1], rr.at[1], d_left)
 
     finish(1, right)
+    finish(2, left)
+    exchanged(1)
     for cols in columns:
-        P1[:, cols] = product(1, 0, TB, cols).astype(BF16)
+        P1[:, cols] = product(1, cols).astype(BF16)
     send(P1.at[pl.ds(H, H)], RL.at[pl.ds(H, H)], sr.at[2], rr.at[2], d_right)
-    finish(2, left)
+    exchanged(2)
     for cols in columns:
-        P2[:, cols] = product(2, 0, TB, cols).astype(BF16)
+        P2[:, cols] = product(2, cols).astype(BF16)
     send(P2.at[pl.ds(0, H)], RR.at[pl.ds(0, H)], sr.at[3], rr.at[3], d_left)
 
     arrived(RU, rr.at[0], sr.at[0])
@@ -403,13 +431,23 @@
     send(P2.at[pl.ds(H, H)], RR.at[pl.ds(H, H)], sr.at[5], rr.at[5], d_left)
 
     finish(3, x)
+    exchanged(3)
     for cols in columns:
-        P3[:, cols] = product(3, 0, TB, cols)
-    arrived(RL.at[pl.ds(H, H)], rr.at[2], sr.at[2])
-    arrived(RR.at[pl.ds(0, H)], rr.at[3], sr.at[3])
-    arrived(RL.at[pl.ds(0, H)], rr.at[4], sr.at[4])
-    arrived(RR.at[pl.ds(H, H)], rr.at[5], sr.at[5])
-    out[...] = (P3[...] + RL[...].astype(F32) + RR[...].astype(F32)).astype(BF16)
+        P3[:, cols] = product(3, cols)
+    upper, lower = pl.ds(0, H), pl.ds(H, H)
+    arrived(RL.at[lower], rr.at[2], sr.at[2])
+    P3[lower, :] += RL[lower, :].astype(F32)
+    arrived(RR.at[upper], rr.at[3], sr.at[3])
+    P3[upper, :] += RR[upper, :].astype(F32)
+    results = []
+    for i, (rows, late, sem) in enumerate(((upper, RL, 4), (lower, RR, 5))):
+        arrived(late.at[rows], rr.at[sem], sr.at[sem])
+        OUT[rows, :] = (P3[rows, :] + late[rows, :].astype(F32)).astype(BF16)
+        result = pltpu.make_async_copy(OUT.at[rows], out.at[rows], loc.at[i])
+        result.start()
+        results.append(result)
+    for result in results:
+        result.wait()
 
     for copy in sent:
         copy.wait_send()
@@ -428,7 +466,7 @@
         kernel,
         out_shape=jax.ShapeDtypeStruct((TB, D), BF16),
         in_specs=[hbm, hbm, vmem, hbm, pl.BlockSpec(memory_space=pltpu.SMEM)],
-        out_specs=vmem,
+        out_specs=hbm,
         scratch_shapes=[
             pltpu.VMEM((ROWS, D), BF16),
             pltpu.VMEM((8 * NR, D), BF16),
@@ -440,6 +478,7 @@
             pltpu.VMEM((ROWS, W), F32),
             pltpu.VMEM((ROWS, W), F32),
             pltpu.VMEM((ROWS, W), F32),
+            pltpu.VMEM((TB, D), BF16),
             pltpu.VMEM((CH, 5 * KB), F32),
             pltpu.VMEM((4, CH, W), BF16),
             pltpu.VMEM((4, TB, 2 * W), BF16),

time: 97 us -> 95.7 us (0.987)
  Pallas kernels: 94.8 us -> 93.5 us
    pallas_call x1, Pallas kernels: 94.8 us -> 93.5 us  [shards(): pl.pallas_call(kernel, out_shape=jax.ShapeDtypeStruct((TB, D), BF16), in_...]
where the time goes in v4:
time: 95.7 us; the launch traced here: 95.5 us
  Pallas kernels  93.5 us (98%)
  local copies, waits for them, and re-layouts  2.06 us (2%)
    pallas_call x1, Pallas kernels, shards(): pl.pallas_call(kernel, out_shape=jax.ShapeDtypeStruct((TB, D), BF16), in_...  93.5 us
    unnamed x1, local copies, waits for them, and re-layouts  2.06 us

profile of v4, /device:TPU:1, one launch (start us, length us, event | category | flops | bytes accessed | tf_op | source)
XLA Modules:
  0.0 95.5 jit_solution(1311058593194918247)
XLA Ops:
  0.0 93.5 %band_attention.1 = bf16[128,3072]{1,0:T(8,128)(2,1)} custom-call(bf16[128,3072]{1,0:T(8,128)(2,1)} %tok.1, bf16[3,3072,384]{2,1,0:T(8,128)(2,1)} %bitcast.2, f32[2,384]{1,0:T(2,128)} %gain.1, bf16[384,3072]{1,0:T(8,128)(2,1)} %wout.1, s32[5,64]{1,0:T(8,128)} %bitcast.3), custom_call_target="tpu_custom_call" | custom-call | flops 14000000000 | bytes 12000000 | tf_op jit(solution)/shard_map/band_attention/pallas_call | solution.py:465
  93.5 2.1 %copy.7 = bf16[128,3072]{1,0:T(8,128)(2,1)} copy(bf16[128,3072]{1,0:T(8,128)(2,1)} %band_attention.1) | data formatting | bytes 1572864
